TPU v7x, 128 devices: a whole 4x4x4 slice. The times are simulated.
128 devices in a mesh: rep: 4 (over x), space: 32 (over z, y, core).
Axes of the slice: x: 4, y: 4, z: 4, core: 2. Of those that a mesh axis runs over, the one named last changes fastest.
Arguments:
- latents: bfloat16 [512, 512, 256], P(('rep', 'space')), may hold values from -6 to 6
- cotangent: bfloat16 [512, 512, 256], P(('rep', 'space')), may hold values from -6 to 6
- w_up: bfloat16 [2, 256, 1024], replicated, may hold values from -0.375 to 0.375
- w_down: bfloat16 [2, 1024, 256], replicated, may hold values from -0.1875 to 0.1875
- depth_w: float32 [2, 7, 256], replicated, may hold values from -2 to 2
- time_table: float32 [1000, 256], replicated, may hold values from -6 to 6
- timesteps: int32 [4], P('rep'), may hold values from 0 to 999
- brick_counts: int32 [128], P(('rep', 'space')), may hold values from 1 to 4, as said below
- send_list: int32 [128, 2, 2], P(('rep', 'space')), may hold values from 0 to 13, as said below
- recv_list: int32 [512, 4], P(('rep', 'space')), may hold values from 0 to 20, as said below
Outputs:
- d_latents: bfloat16 [512, 512, 256], P(('rep', 'space'))
- grad_up: float32 [2, 256, 1024], P(None, None, 'rep')
- grad_down: float32 [2, 1024, 256], P(None, 'rep')
- grad_depth: float32 [2, 7, 256], P(None, None, 'rep')
Inputs may be any that keep to these rules, and one draw needn't show every extreme that they name: `brick_counts`: some device of every scene holds 4 bricks and some holds one. `send_list`: entry 4 s + f names face f of local slot s; list 0 goes to the device below along space, list 1 to the device above. `recv_list`: 0 means no neighbour, 1 + 4 s + f face f of local slot s, 17 + e entry e received from the device below, 19 + e entry e from the device above. Empty slots have 0 on every side. Whenever a slot names a face across a side, the brick of that face names this slot's facing face across the opposite side.
All inputs are finite; a program needn't handle non-finite values.
Results may differ from a plain program's by a relative error of at most 0.035.
Values may be sent and summed in bfloat16 or wider, within the bound.
A program may use at most 128 MiB of HBM per device.

v0:
```python
import math
import jax
import jax.numpy as jnp
from jax import lax
from jax.sharding import PartitionSpec as P

E = 8
CUBIC = 0.044715
ROOT = math.sqrt(2.0 / math.pi)
FORWARD_ORDER = (0, 1, 2, 3, 4, 5, 6)
MIRROR_ORDER = (0, 2, 1, 4, 3, 6, 5)


def from_behind(value, axis, steps):
    count = lax.axis_size(axis)
    initial, last = (max(0, -steps), min(count, count - steps))
    return lax.ppermute(value, axis, [(source, source + steps) for source in range(initial, last)])


def gelu_tanh(values):
    return 0.5 * values * (1.0 + jnp.tanh(ROOT * (values + CUBIC * values * values * values)))


def gelu_slope(values):
    inner = jnp.tanh(ROOT * (values + CUBIC * values * values * values))
    return 0.5 * (1.0 + inner) + 0.5 * values * (1.0 - inner * inner) * ROOT * (
        1.0 + 3.0 * CUBIC * values * values
    )


def planes_of(fields):
    count = fields.shape[0]
    cube = fields.reshape(count, E, E, E, fields.shape[-1])
    stacked = jnp.stack([cube[:, 0], cube[:, E - 1], cube[:, :, 0], cube[:, :, E - 1]], axis=1)
    return stacked.reshape(count * 4, E * E, fields.shape[-1])


def neighbours(field, ghosts):
    count = field.shape[0]
    width = field.shape[-1]
    cube = field.reshape(count, E, E, E, width).astype(jnp.float32)
    sides = ghosts.reshape(count, 4, E, E, width).astype(jnp.float32)
    along_x = jnp.concatenate([sides[:, 0:1], cube, sides[:, 1:2]], axis=1)
    along_y = jnp.concatenate([sides[:, 2][:, :, None], cube, sides[:, 3][:, :, None]], axis=2)
    along_z = jnp.pad(cube, ((0, 0), (0, 0), (0, 0), (1, 1), (0, 0)))
    pieces = [
        cube,
        along_x[:, :-2],
        along_x[:, 2:],
        along_y[:, :, :-2],
        along_y[:, :, 2:],
        along_z[:, :, :, :-2],
        along_z[:, :, :, 2:],
    ]
    return [piece.reshape(-1, width) for piece in pieces]


def combine(fields, weights, order):
    total = weights[order[0]][None, :] * fields[0]
    for index in range(1, 7):
        total = total + weights[order[index]][None, :] * fields[index]
    return total


def trade_faces(fields, sends, recvs):
    copies, bricks, voxels, channels = fields.shape
    planes = planes_of(fields.reshape(copies * bricks, voxels, channels)).reshape(
        copies, bricks * 4, E * E, channels
    )
    outgoing = planes[:, sends.reshape(-1)].reshape(copies, 2, sends.shape[1], E * E, channels)
    from_lower = from_behind(outgoing[:, 1], "space", 1)
    from_upper = from_behind(outgoing[:, 0], "space", -1)
    blank = jnp.zeros((copies, 1, E * E, channels), jnp.bfloat16)
    face_pool = jnp.concatenate([blank, planes, from_lower, from_upper], axis=1)
    return face_pool[:, recvs.reshape(-1)].reshape(copies, bricks, 4, E * E, channels)


def on_device(
    latents,
    cotangent,
    w_up,
    w_down,
    depth_w,
    time_table,
    timesteps,
    brick_counts,
    send_list,
    recv_list,
):
    bricks, voxels, channels = latents.shape
    blocks = w_up.shape[0]
    sends = send_list[0]
    occupied = (jnp.arange(bricks, dtype=jnp.int32) < brick_counts[0]).astype(jnp.float32)[
        :, None, None
    ]
    time_shift = time_table[timesteps[0]]
    field = (latents.astype(jnp.float32) * occupied).astype(jnp.bfloat16)
    saved = []
    for block in range(blocks):
        ghosts = trade_faces(field[None], sends, recv_list)[0]
        near = neighbours(field, ghosts)
        activation = (combine(near, depth_w[block], FORWARD_ORDER) + time_shift[None, :]).astype(
            jnp.bfloat16
        )
        preact = jnp.dot(activation, w_up[block], preferred_element_type=jnp.float32)
        hidden = gelu_tanh(preact).astype(jnp.bfloat16)
        summed = field.reshape(-1, channels).astype(jnp.float32) + jnp.dot(
            hidden, w_down[block], preferred_element_type=jnp.float32
        )
        saved.append((field, ghosts, activation, preact, hidden))
        field = (summed.reshape(bricks, voxels, channels) * occupied).astype(jnp.bfloat16)
    grad = (cotangent.astype(jnp.float32) * occupied).astype(jnp.bfloat16)
    parts_up = [None] * blocks
    parts_down = [None] * blocks
    parts_depth = [None] * blocks
    contract_rows = (((0,), (0,)), ((), ()))
    contract_cols = (((1,), (1,)), ((), ()))
    for block in range(blocks - 1, -1, -1):
        field_in, ghosts_in, activation, preact, hidden = saved[block]
        flat_grad = grad.reshape(-1, channels)
        parts_down[block] = lax.dot_general(
            hidden, flat_grad, contract_rows, preferred_element_type=jnp.float32
        )
        d_hidden = lax.dot_general(
            flat_grad, w_down[block], contract_cols, preferred_element_type=jnp.float32
        )
        d_preact = (d_hidden * gelu_slope(preact)).astype(jnp.bfloat16)
        parts_up[block] = lax.dot_general(
            activation, d_preact, contract_rows, preferred_element_type=jnp.float32
        )
        d_act = lax.dot_general(
            d_preact, w_up[block], contract_cols, preferred_element_type=jnp.float32
        ).astype(jnp.bfloat16)
        d_field = d_act.reshape(bricks, voxels, channels)
        ghosts_grad = trade_faces(d_field[None], sends, recv_list)[0]
        near_in = neighbours(field_in, ghosts_in)
        d_wide = d_act.astype(jnp.float32)
        parts_depth[block] = jnp.stack([jnp.sum(piece * d_wide, axis=0) for piece in near_in])
        back = combine(neighbours(d_field, ghosts_grad), depth_w[block], MIRROR_ORDER)
        total = flat_grad.astype(jnp.float32) + back
        grad = (total.reshape(bricks, voxels, channels) * occupied).astype(jnp.bfloat16)
    local_up = jnp.stack(parts_up)
    local_down = jnp.stack(parts_down)
    local_depth = jnp.stack(parts_depth)
    whole = (
        lax.psum(local_up.astype(jnp.bfloat16), "space").astype(jnp.float32),
        lax.psum(local_down.astype(jnp.bfloat16), "space").astype(jnp.float32),
        lax.psum(local_depth.astype(jnp.bfloat16), "space").astype(jnp.float32),
    )
    sum_up, sum_down, sum_depth = (
        lax.psum_scatter(
            whole[0].astype(jnp.bfloat16), "rep", scatter_dimension=2, tiled=True
        ).astype(jnp.float32),
        lax.psum_scatter(
            whole[1].astype(jnp.bfloat16), "rep", scatter_dimension=1, tiled=True
        ).astype(jnp.float32),
        lax.psum_scatter(
            whole[2].astype(jnp.bfloat16), "rep", scatter_dimension=2, tiled=True
        ).astype(jnp.float32),
    )
    scale = 1.0 / math.sqrt(bricks * lax.axis_size("rep") * lax.axis_size("space") * voxels)
    return (grad, sum_up * scale, sum_down * scale, sum_depth * scale)


def solution(mesh):
    return jax.shard_map(
        on_device,
        mesh=mesh,
        in_specs=(
            P(("rep", "space"), None, None),
            P(("rep", "space"), None, None),
            P(),
            P(),
            P(),
            P(),
            P("rep"),
            P(("rep", "space")),
            P(("rep", "space"), None, None),
            P(("rep", "space"), None),
        ),
        out_specs=(
            P(("rep", "space"), None, None),
            P(None, None, "rep"),
            P(None, "rep", None),
            P(None, None, "rep"),
        ),
        check_vma=False,
    )
```

profile of v0, /device:TPU:1, one launch (start us, length us, event | category | flops | bytes accessed | tf_op | source)
XLA Modules:
  0.0 312.6 jit_solution(17737770641990076478)
XLA Ops:
  8.0 3.4 %multiply_convert_fusion.6 = (bf16[4,512,256]{2,1,0:T(8,128)(2,1)}, bf16[4,512,256]{2,1,0:T(8,128)(2,1)S(1)}) fusion(bf16[4,512,256]{2,1,0:T(8,128)(2,1)} %param.11, f32[4]{0:T(128)S(1)} %compare_convert_fusion, bf16[4,512,256]{2,1,0:T(8,128)(2,1)} %param.10), kind=kLoop, calls=%fused_computation.163 | loop fusion | flops 3145728 | bytes 4194320 | tf_op jit(solution)/shard_map/convert_element_type | solution.py:112
  11.7 0.6 gather_fusion
  12.3 4.6 %collective-permute-start = (bf16[1,2,64,256]{3,2,1,0:T(8,128)(2,1)S(1)}, bf16[1,2,64,256]{3,2,1,0:T(8,128)(2,1)S(1)}, u32[]{:S(2)}, u32[]{:S(2)}) collective-permute-start(bf16[1,2,64,256]{3,2,1,0:T(8,128)(2,1)S(1)} %get-tuple-element.97), channel_id=1, source_target_pairs={{0,1},{1,2},{2,3},{3,4},{4,5},{5,6},{6,7},{7,8},{8,9},{9,10},{10,1... | collective-permute-start | bytes 196616 | tf_op jit(solution)/shard_map/ppermute | solution.py:17
  16.9 1.9 collective-permute-start.1
  18.8 1.6 convert_element_type.165
  21.3 1.2 collective-permute-done.1
  22.6 0.6 gather_fusion.1
  23.4 1.4 copy-done.22
  24.8 1.4 pad_maximum_fusion.15
  26.3 1.2 fusion.63
  27.6 0.6 copy-done.11
  28.3 0.6 copy-done.13
  28.9 0.7 copy-done.15
  29.6 0.6 copy-done.17
  30.2 0.6 copy-done.19
  30.8 1.3 fusion.81
  32.3 3.0 convolution_add_fusion
  35.4 1.8 fusion.97
  37.2 0.6 gather_fusion.2
  37.8 2.5 collective-permute-start.2
  40.3 2.1 collective-permute-start.3
  42.6 3.2 %collective-permute-done.3 = bf16[1,2,64,256]{3,2,1,0:T(8,128)(2,1)S(1)} collective-permute-done((bf16[1,2,64,256]{3,2,1,0:T(8,128)(2,1)S(1)}, bf16[1,2,64,256]{3,2,1,0:T(8,128)(2,1)S(1)}, u32[]{:S(2)}, u32[]{:S(2)}) %collective-permute-start.3) | collective-permute-done | bytes 65568 | tf_op jit(solution)/shard_map/ppermute | solution.py:17
  45.8 1.0 maximum_bitcast_fusion.1
  46.8 1.7 gather_fusion.3
  48.7 1.4 copy-done.21
  50.1 1.7 pad_maximum_fusion.11
  53.6 2.2 fusion.22
  55.9 1.3 fusion.76
  57.5 0.3 copy-done.41
  57.8 5.9 %fusion.8 = bf16[2048,1024]{1,0:T(8,128)(2,1)S(1)} fusion(f32[2048,1024]{1,0:T(8,128)S(1)} %fusion.76, bf16[2048,256]{1,0:T(8,128)(2,1)S(1)} %bitcast.382, bf16[2,1024,256]{2,1,0:T(8,128)(2,1)S(1)} %copy-done.41), kind=kOutput, calls=%fused_computation.20 | convolution fusion | flops 1113587712 | bytes 14155776 | tf_op jit(solution)/shard_map/dot_general | solution.py:124
  63.7 4.2 %fusion.38 = (bf16[256]{0:T(256)(128)(2,1)S(1)}, bf16[256]{0:T(256)(128)(2,1)S(1)}, bf16[256]{0:T(256)(128)(2,1)S(1)}, bf16[256]{0:T(256)(128)(2,1)S(1)}, bf16[2...) fusion(f32[4,8,8,8,256]{4,3,2,1,0:T(8,128)S(1)} %copy.124, ...), kind=kOutput, calls=%fused_computation.80 | convolution fusion | flops 1083701504 | bytes 20459008 | tf_op jit(solution)/shard_map/dot_general | solution.py:131
  68.0 1.0 copy-done.7
  69.1 0.6 gather_fusion.4
  69.7 1.9 collective-permute-start.4
  71.6 2.8 collective-permute-start.5
  74.4 6.1 %fusion.71 = bf16[1,1024,256]{2,1,0:T(8,128)(2,1)} fusion(bf16[2048,256]{1,0:T(8,128)(2,1)S(1)} %bitcast.383, f32[2048,1024]{1,0:T(8,128)} %copy-done.3), kind=kOutput, calls=%fused_computation.168 | convolution fusion | flops 1092878336 | bytes 9961472 | tf_op jit(solution)/shard_map/dot_general | solution.py:121
  80.5 1.6 convert_element_type.181
  82.2 1.0 maximum_bitcast_fusion.2
  83.2 1.7 gather_fusion.5
  85.1 1.4 copy-done.23
  86.5 1.7 pad_maximum_fusion.7
  88.2 2.2 fusion.31
  90.5 3.6 %fusion.74 = bf16[1,1024,256]{2,1,0:T(8,128)(2,1)S(1)} fusion(bf16[2048,256]{1,0:T(8,128)(2,1)S(1)} %fusion.31, f32[2048,1024]{1,0:T(8,128)S(1)} %bitcast.361), kind=kOutput, calls=%fused_computation.171 | convolution fusion | flops 1092878336 | bytes 9961472 | tf_op jit(solution)/shard_map/dot_general | solution.py:121
  94.2 5.9 %fusion.13 = bf16[2048,1024]{1,0:T(8,128)(2,1)S(1)} fusion(f32[2048,1024]{1,0:T(8,128)S(1)} %bitcast.361, bf16[2048,256]{1,0:T(8,128)(2,1)S(1)} %fusion.31, bf16[2,1024,256]{2,1,0:T(8,128)(2,1)S(1)} %copy-done.42), kind=kOutput, calls=%fused_computation.25 | convolution fusion | flops 1113587712 | bytes 14155776 | tf_op jit(solution)/shard_map/dot_general | solution.py:124
  100.2 5.9 %fusion.52 = (bf16[256]{0:T(256)(128)(2,1)S(1)}, bf16[256]{0:T(256)(128)(2,1)S(1)}, bf16[256]{0:T(256)(128)(2,1)S(1)}, bf16[256]{0:T(256)(128)(2,1)S(1)}, bf16[2...) fusion(f32[4,8,8,8,256]{4,3,2,1,0:T(8,128)S(1)} %copy-done.12, ...), kind=kOutput, calls=%fused_computation.94 | convolution fusion | flops 1090517248 | bytes 20459008 | tf_op jit(solution)/shard_map/dot_general | solution.py:131
  106.4 0.7 reshape.436
  107.2 1.1 pad_maximum_fusion.17
  108.4 4.3 %fusion.73 = bf16[1,256,1024]{2,1,0:T(8,128)(2,1)} fusion(bf16[2048,256]{1,0:T(8,128)(2,1)S(1)} %copy-done.27, bf16[2048,1024]{1,0:T(8,128)(2,1)} %copy-done.32), kind=kOutput, calls=%fused_computation.170 | convolution fusion | flops 1074003968 | bytes 5767168 | tf_op jit(solution)/shard_map/dot_general | solution.py:128
  113.1 0.6 gather_fusion.6
  113.7 3.1 %collective-permute-start.6 = (bf16[1,2,64,256]{3,2,1,0:T(8,128)(2,1)S(1)}, bf16[1,2,64,256]{3,2,1,0:T(8,128)(2,1)S(1)}, u32[]{:S(2)}, u32[]{:S(2)}) collective-permute-start(bf16[1,2,64,256]{3,2,1,0:T(8,128)(2,1)S(1)} %get-tuple-element.91), channel_id=1, source_target_pairs={{0,1},{1,2},{2,3},{3,4},{4,5},{5,6},{6,7},{7,8},{8,9},{9,10},{10,1... | collective-permute-start | bytes 196616 | tf_op jit(solution)/shard_map/ppermute | solution.py:17
  116.9 2.2 collective-permute-start.7
  119.1 3.8 %fusion.72 = bf16[1,256,1024]{2,1,0:T(8,128)(2,1)S(1)} fusion(bf16[2048,256]{1,0:T(8,128)(2,1)} %get-tuple-element.34, bf16[2048,1024]{1,0:T(8,128)(2,1)} %copy-done.44), kind=kOutput, calls=%fused_computation.169 | convolution fusion | flops 1074003968 | bytes 5767168 | tf_op jit(solution)/shard_map/dot_general | solution.py:128
  122.9 1.1 pad_maximum_fusion.16
  124.1 6.8 %reduce-scatter.10.cloned.1.call-done = bf16[64,14]{1,0:T(8,128)(2,1)} async-done(((bf16[256,14]{1,0:T(8,128)(2,1)}), bf16[64,14]{1,0:T(8,128)(2,1)}) %reduce-scatter.10.cloned.1.call-update) | async-done | bytes 1808
  130.8 0.8 reshape.437
  131.7 65.2 %psum.26 = bf16[2,7,64]{2,1,0:T(8,128)(2,1)S(1)} all-reduce(bf16[2,7,64]{2,1,0:T(8,128)(2,1)S(1)} %copy.135), channel_id=1, replica_groups=mesh['rep'=4,'space'=32] {'space'}, use_global_device_ids=true, to_apply=%region_18.19 | all-reduce | flops 896 | bytes 3584 | tf_op jit(solution)/shard_map/psum | solution.py:148
  196.9 0.6 copy.133
  197.5 1.0 maximum_bitcast_fusion.3
  198.5 1.7 gather_fusion.7
  200.4 1.4 pad_maximum_fusion.3
  201.9 1.1 fusion.45
  203.1 1.3 multiply_convert_fusion.3
  204.4 99.6 %all-reduce.7.cloned.1.call-done = (bf16[2,256,256]{2,1,0:T(8,128)(2,1)}, bf16[2,256,256]{2,1,0:T(8,128)(2,1)}) async-done(((bf16[2,256,256]{2,1,0:T(8,128)(2,1)}, bf16[2,256,256]{2,1,0:T(8,128)(2,1)}), (bf16[2,256,256]{2,1,0:T(8,128)(2,1)}, bf16[2,256,256]{2,1,0:T(8,128)(2,1)})) %all-reduce.7.cloned.1.call-update) | async-done | bytes 524304 | tf_op jit(solution)/shard_map/psum | solution.py:146
  304.0 2.1 convert_multiply_fusion.17
  (172 shorter events, 5.5 us)
Async XLA Ops:
  7.2 14.1 %copy-start = (f32[1000,256]{1,0:T(8,128)S(1)}, f32[1000,256]{1,0:T(8,128)}, u32[]{:S(2)}) copy-start(f32[1000,256]{1,0:T(8,128)} %param.15) | copy-start | bytes 3072004
  7.2 123.6 %reduce-scatter.10.cloned.1.call-start = ((), (), s32[]{:S(2)}) async-start(), calls=%async_computation.5 | async-start | bytes 81920
  8.0 3.5 %copy-start.43 = (s32[1,2,2]{2,1,0:T(2,128)S(1)}, s32[1,2,2]{2,1,0:T(2,128)}, u32[]{:S(2)}) copy-start(s32[1,2,2]{2,1,0:T(2,128)} %param.18) | copy-start | bytes 52
  11.4 14.9 %copy-start.4 = (bf16[4,512,256]{2,1,0:T(8,128)(2,1)}, bf16[4,512,256]{2,1,0:T(8,128)(2,1)S(1)}, u32[]{:S(2)}) copy-start(bf16[4,512,256]{2,1,0:T(8,128)(2,1)S(1)} %get-tuple-element.114) | copy-start | bytes 3145732
  11.7 9.4 %copy-start.39 = (s32[4,4]{1,0:T(4,128)S(1)}, s32[4,4]{1,0:T(4,128)}, u32[]{:S(2)}) copy-start(s32[4,4]{1,0:T(4,128)} %param.19) | copy-start | bytes 196
  11.7 9.5 %copy-start.38 = (f32[2,7,256]{2,0,1:T(2,128)S(1)}, f32[2,7,256]{2,0,1:T(2,128)}, u32[]{:S(2)}) copy-start(f32[2,7,256]{2,0,1:T(2,128)} %param.14) | copy-start | bytes 43012
  12.3 9.0 %collective-permute-start = (bf16[1,2,64,256]{3,2,1,0:T(8,128)(2,1)S(1)}, bf16[1,2,64,256]{3,2,1,0:T(8,128)(2,1)S(1)}, u32[]{:S(2)}, u32[]{:S(2)}) collective-permute-start(bf16[1,2,64,256]{3,2,1,0:T(8,128)(2,1)S(1)} %get-tuple-element.97), channel_id=1, source_target_pairs={{0,1},{1,2},{2,3},{3,4},{4,5},{5,6},{6,7},{7,8},{8,9},{9,10},{10,1... | collective-permute-start | bytes 196616 | tf_op jit(solution)/shard_map/ppermute | solution.py:17
  16.9 5.6 %collective-permute-start.1 = (bf16[1,2,64,256]{3,2,1,0:T(8,128)(2,1)S(1)}, bf16[1,2,64,256]{3,2,1,0:T(8,128)(2,1)S(1)}, u32[]{:S(2)}, u32[]{:S(2)}) collective-permute-start(bf16[1,2,64,256]{3,2,1,0:T(8,128)(2,1)S(1)} %get-tuple-element.98), channel_id=1, source_target_pairs={{1,0},{2,1},{3,2},{4,3},{5,4},{6,5},{7,6},{8,7},{9,8},{10,9},{11,1... | collective-permute-start | bytes 196616 | tf_op jit(solution)/shard_map/ppermute | solution.py:17
  23.2 1.6 copy-start.22
  26.2 1.4 copy-start.9
  26.2 2.0 copy-start.11
  26.2 2.6 copy-start.13
  26.2 3.3 %copy-start.15 = (f32[4,8,8,8,256]{4,3,2,1,0:T(8,128)}, f32[4,8,8,8,256]{4,3,2,1,0:T(8,128)S(1)}, u32[]{:S(2)}) copy-start(f32[4,8,8,8,256]{4,3,2,1,0:T(8,128)S(1)} %get-tuple-element.56) | copy-start | bytes 6291460
  26.3 3.9 %copy-start.17 = (f32[4,8,8,8,256]{4,3,2,1,0:T(8,128)}, f32[4,8,8,8,256]{4,3,2,1,0:T(8,128)S(1)}, u32[]{:S(2)}) copy-start(f32[4,8,8,8,256]{4,3,2,1,0:T(8,128)S(1)} %get-tuple-element.57) | copy-start | bytes 6291460
  26.3 4.5 %copy-start.19 = (f32[4,8,8,8,256]{4,3,2,1,0:T(8,128)}, f32[4,8,8,8,256]{4,3,2,1,0:T(8,128)S(1)}, u32[]{:S(2)}) copy-start(f32[4,8,8,8,256]{4,3,2,1,0:T(8,128)S(1)} %get-tuple-element.58) | copy-start | bytes 6291460
  26.3 4.5 %copy-start.33 = (bf16[2,256,1024]{2,1,0:T(8,128)(2,1)S(1)}, bf16[2,256,1024]{2,1,0:T(8,128)(2,1)}, u32[]{:S(2)}) copy-start(bf16[2,256,1024]{2,1,0:T(8,128)(2,1)} %param.12) | copy-start | bytes 3145732
  30.8 1.3 copy-start.5
  30.8 1.5 copy-start.40
  32.1 3.3 %copy-start.2 = (f32[2048,1024]{1,0:T(8,128)}, f32[2048,1024]{1,0:T(8,128)S(1)}, u32[]{:S(2)}) copy-start(f32[2048,1024]{1,0:T(8,128)S(1)} %fusion.81) | copy-start | bytes 25165828
  37.8 4.8 %collective-permute-start.2 = (bf16[1,2,64,256]{3,2,1,0:T(8,128)(2,1)S(1)}, bf16[1,2,64,256]{3,2,1,0:T(8,128)(2,1)S(1)}, u32[]{:S(2)}, u32[]{:S(2)}) collective-permute-start(bf16[1,2,64,256]{3,2,1,0:T(8,128)(2,1)S(1)} %get-tuple-element.95), channel_id=1, source_target_pairs={{0,1},{1,2},{2,3},{3,4},{4,5},{5,6},{6,7},{7,8},{8,9},{9,10},{10,1... | collective-permute-start | bytes 196616 | tf_op jit(solution)/shard_map/ppermute | solution.py:17
  40.3 5.6 %collective-permute-start.3 = (bf16[1,2,64,256]{3,2,1,0:T(8,128)(2,1)S(1)}, bf16[1,2,64,256]{3,2,1,0:T(8,128)(2,1)S(1)}, u32[]{:S(2)}, u32[]{:S(2)}) collective-permute-start(bf16[1,2,64,256]{3,2,1,0:T(8,128)(2,1)S(1)} %get-tuple-element.96), channel_id=1, source_target_pairs={{1,0},{2,1},{3,2},{4,3},{5,4},{6,5},{7,6},{8,7},{9,8},{10,9},{11,1... | collective-permute-start | bytes 196616 | tf_op jit(solution)/shard_map/ppermute | solution.py:17
  48.5 1.6 copy-start.21
  53.6 2.2 copy-start.34
  55.9 1.3 copy-start.26
  55.9 1.6 copy-start.28
  55.9 1.9 copy-start.41
  57.2 6.5 %copy-start.3 = (f32[2048,1024]{1,0:T(8,128)}, f32[2048,1024]{1,0:T(8,128)S(1)}, u32[]{:S(2)}) copy-start(f32[2048,1024]{1,0:T(8,128)S(1)} %fusion.76) | copy-start | bytes 25165828
  63.7 4.3 %copy-start.32 = (bf16[2048,1024]{1,0:T(8,128)(2,1)}, bf16[2048,1024]{1,0:T(8,128)(2,1)S(1)}, u32[]{:S(2)}) copy-start(bf16[2048,1024]{1,0:T(8,128)(2,1)S(1)} %fusion.8) | copy-start | bytes 12582916
  68.0 1.0 copy-start.7
  68.0 6.4 %copy-start.29 = (bf16[4,512,256]{2,1,0:T(8,128)(2,1)S(1)}, bf16[4,512,256]{2,1,0:T(8,128)(2,1)}, u32[]{:S(2)}) copy-start(bf16[4,512,256]{2,1,0:T(8,128)(2,1)} %get-tuple-element.113) | copy-start | bytes 3145732
  69.7 12.5 %collective-permute-start.4 = (bf16[1,2,64,256]{3,2,1,0:T(8,128)(2,1)S(1)}, bf16[1,2,64,256]{3,2,1,0:T(8,128)(2,1)S(1)}, u32[]{:S(2)}, u32[]{:S(2)}) collective-permute-start(bf16[1,2,64,256]{3,2,1,0:T(8,128)(2,1)S(1)} %get-tuple-element.93), channel_id=1, source_target_pairs={{0,1},{1,2},{2,3},{3,4},{4,5},{5,6},{6,7},{7,8},{8,9},{9,10},{10,1... | collective-permute-start | bytes 196616 | tf_op jit(solution)/shard_map/ppermute | solution.py:17
  71.6 8.9 %copy-start.8 = (bf16[2048,256]{1,0:T(8,128)(2,1)S(1)}, bf16[2048,256]{1,0:T(8,128)(2,1)}, u32[]{:S(2)}) copy-start(bf16[2048,256]{1,0:T(8,128)(2,1)} %copy-done.7) | copy-start | bytes 3145732
  71.6 10.5 %collective-permute-start.5 = (bf16[1,2,64,256]{3,2,1,0:T(8,128)(2,1)S(1)}, bf16[1,2,64,256]{3,2,1,0:T(8,128)(2,1)S(1)}, u32[]{:S(2)}, u32[]{:S(2)}) collective-permute-start(bf16[1,2,64,256]{3,2,1,0:T(8,128)(2,1)S(1)} %get-tuple-element.94), channel_id=1, source_target_pairs={{1,0},{2,1},{3,2},{4,3},{5,4},{6,5},{7,6},{8,7},{9,8},{10,9},{11,1... | collective-permute-start | bytes 196616 | tf_op jit(solution)/shard_map/ppermute | solution.py:17
  84.9 1.6 copy-start.23
  86.4 4.0 %slice-start = ((s8[8388608]{0:T(1024)(128)(4,1)}), s8[4194304]{0:T(1024)(128)(4,1)S(1)}, s32[]{:S(2)}) async-start(s8[8388608]{0:T(1024)(128)(4,1)} %bitcast.360), calls=%async_computation.7 | async-start | bytes 8388608
  88.2 2.3 slice-start.1
  90.5 3.6 %copy-start.30 = (bf16[2048,256]{1,0:T(8,128)(2,1)}, bf16[2048,256]{1,0:T(8,128)(2,1)S(1)}, u32[]{:S(2)}) copy-start(bf16[2048,256]{1,0:T(8,128)(2,1)S(1)} %fusion.31) | copy-start | bytes 3145732
  90.5 3.6 %copy-start.42 = (bf16[2,1024,256]{2,1,0:T(8,128)(2,1)S(1)}, bf16[2,1024,256]{2,1,0:T(8,128)(2,1)}, u32[]{:S(2)}) copy-start(bf16[2,1024,256]{2,1,0:T(8,128)(2,1)} %param.13) | copy-start | bytes 3145732
  94.1 6.0 %copy-start.6 = (bf16[4,512,256]{2,1,0:T(8,128)(2,1)S(1)}, bf16[4,512,256]{2,1,0:T(8,128)(2,1)}, u32[]{:S(2)}) copy-start(bf16[4,512,256]{2,1,0:T(8,128)(2,1)} %copy-done.4) | copy-start | bytes 3145732
  94.1 6.0 %copy-start.10 = (f32[4,8,8,8,256]{4,3,2,1,0:T(8,128)S(1)}, f32[4,8,8,8,256]{4,3,2,1,0:T(8,128)}, u32[]{:S(2)}) copy-start(f32[4,8,8,8,256]{4,3,2,1,0:T(8,128)} %copy-done.9) | copy-start | bytes 6291460
  94.1 6.0 %copy-start.12 = (f32[4,8,8,8,256]{4,3,2,1,0:T(8,128)S(1)}, f32[4,8,8,8,256]{4,3,2,1,0:T(8,128)}, u32[]{:S(2)}) copy-start(f32[4,8,8,8,256]{4,3,2,1,0:T(8,128)} %copy-done.11) | copy-start | bytes 6291460
  94.1 6.0 %copy-start.14 = (f32[4,8,8,8,256]{4,3,2,1,0:T(8,128)S(1)}, f32[4,8,8,8,256]{4,3,2,1,0:T(8,128)}, u32[]{:S(2)}) copy-start(f32[4,8,8,8,256]{4,3,2,1,0:T(8,128)} %copy-done.13) | copy-start | bytes 6291460
  94.1 6.0 %copy-start.16 = (f32[4,8,8,8,256]{4,3,2,1,0:T(8,128)S(1)}, f32[4,8,8,8,256]{4,3,2,1,0:T(8,128)}, u32[]{:S(2)}) copy-start(f32[4,8,8,8,256]{4,3,2,1,0:T(8,128)} %copy-done.15) | copy-start | bytes 6291460
  94.1 6.0 %copy-start.18 = (f32[4,8,8,8,256]{4,3,2,1,0:T(8,128)S(1)}, f32[4,8,8,8,256]{4,3,2,1,0:T(8,128)}, u32[]{:S(2)}) copy-start(f32[4,8,8,8,256]{4,3,2,1,0:T(8,128)} %copy-done.17) | copy-start | bytes 6291460
  94.2 6.0 %copy-start.20 = (f32[4,8,8,8,256]{4,3,2,1,0:T(8,128)S(1)}, f32[4,8,8,8,256]{4,3,2,1,0:T(8,128)}, u32[]{:S(2)}) copy-start(f32[4,8,8,8,256]{4,3,2,1,0:T(8,128)} %copy-done.19) | copy-start | bytes 6291460
  94.2 6.0 %copy-start.35 = (bf16[2,256,1024]{2,1,0:T(8,128)(2,1)S(1)}, bf16[2,256,1024]{2,1,0:T(8,128)(2,1)}, u32[]{:S(2)}) copy-start(bf16[2,256,1024]{2,1,0:T(8,128)(2,1)} %param.12) | copy-start | bytes 3145732
  100.2 5.9 %copy-start.44 = (bf16[2048,1024]{1,0:T(8,128)(2,1)}, bf16[2048,1024]{1,0:T(8,128)(2,1)S(1)}, u32[]{:S(2)}) copy-start(bf16[2048,1024]{1,0:T(8,128)(2,1)S(1)} %fusion.13) | copy-start | bytes 12582916
  100.2 7.0 %copy-start.36 = (bf16[1,1024,256]{2,1,0:T(8,128)(2,1)S(1)}, bf16[1,1024,256]{2,1,0:T(8,128)(2,1)}, u32[]{:S(2)}) copy-start(bf16[1,1024,256]{2,1,0:T(8,128)(2,1)} %fusion.71) | copy-start | bytes 1572868
  106.1 2.3 copy-start.27
  107.2 95.9 %reduce-scatter.8.cloned.1.call-start = ((), (), s32[]{:S(2)}) async-start(), calls=%async_computation.4 | async-start | bytes 1310720 | tf_op jit(solution)/shard_map/reduce_scatter | solution.py:154
  108.3 94.8 %reduce-scatter.6.cloned.1.call-start = ((), (), s32[]{:S(2)}) async-start(), calls=%async_computation.3 | async-start | bytes 1310720 | tf_op jit(solution)/shard_map/reduce_scatter | solution.py:151
  108.4 4.4 %copy-start.24 = (bf16[2048,256]{1,0:T(8,128)(2,1)S(1)}, bf16[2048,256]{1,0:T(8,128)(2,1)}, u32[]{:S(2)}) copy-start(bf16[2048,256]{1,0:T(8,128)(2,1)} %get-tuple-element.115) | copy-start | bytes 3145732
  113.7 83.8 %collective-permute-start.6 = (bf16[1,2,64,256]{3,2,1,0:T(8,128)(2,1)S(1)}, bf16[1,2,64,256]{3,2,1,0:T(8,128)(2,1)S(1)}, u32[]{:S(2)}, u32[]{:S(2)}) collective-permute-start(bf16[1,2,64,256]{3,2,1,0:T(8,128)(2,1)S(1)} %get-tuple-element.91), channel_id=1, source_target_pairs={{0,1},{1,2},{2,3},{3,4},{4,5},{5,6},{6,7},{7,8},{8,9},{9,10},{10,1... | collective-permute-start | bytes 196616 | tf_op jit(solution)/shard_map/ppermute | solution.py:17
  116.9 80.6 %collective-permute-start.7 = (bf16[1,2,64,256]{3,2,1,0:T(8,128)(2,1)S(1)}, bf16[1,2,64,256]{3,2,1,0:T(8,128)(2,1)S(1)}, u32[]{:S(2)}, u32[]{:S(2)}) collective-permute-start(bf16[1,2,64,256]{3,2,1,0:T(8,128)(2,1)S(1)} %get-tuple-element.92), channel_id=1, source_target_pairs={{1,0},{2,1},{3,2},{4,3},{5,4},{6,5},{7,6},{8,7},{9,8},{10,9},{11,1... | collective-permute-start | bytes 196616 | tf_op jit(solution)/shard_map/ppermute | solution.py:17
  119.1 3.9 %copy-start.37 = (bf16[1,256,1024]{2,1,0:T(8,128)(2,1)S(1)}, bf16[1,256,1024]{2,1,0:T(8,128)(2,1)}, u32[]{:S(2)}) copy-start(bf16[1,256,1024]{2,1,0:T(8,128)(2,1)} %fusion.73) | copy-start | bytes 1572868
  124.0 180.0 %all-reduce.7.cloned.1.call-start = ((), (), s32[]{:S(2)}) async-start(), calls=%async_computation.6 | async-start | bytes 1048576 | tf_op jit(solution)/shard_map/psum | solution.py:146
  200.4 1.5 copy-start.25
  200.4 1.5 copy-start.31
  203.1 103.0 %copy-start.1 = (f32[1000,256]{1,0:T(8,128)S(1)}, f32[1000,256]{1,0:T(8,128)}, u32[]{:S(2)}) copy-start(f32[1000,256]{1,0:T(8,128)} %param.15) | copy-start | bytes 3072004
Sparse Core Ops, SparseCore 0:
  107.3 23.4 reduce-scatter.9
  133.3 24.0 reduce-scatter.7
  160.4 23.1 reduce-scatter.5
  203.2 100.7 all-reduce.6
where the time goes:
time: 314 us; the launch traced here: 313 us
  waiting for transfers between devices  111 us (35%)
  blocking collectives  65.2 us (21%)
  matrix products  45.3 us (14%)
  other arithmetic  31 us (10%)
  local copies, waits for them, and re-layouts  22.7 us (7%)
  starting transfers between devices  21.2 us (7%)
  between operations  16.4 us (5%)
    psum x1, waiting for transfers between devices, on_device(): lax.psum(local_up.astype(jnp.bfloat16), 'space').astype(jnp.float32)  99.6 us
    psum x1, blocking collectives, on_device(): lax.psum(local_depth.astype(jnp.bfloat16), 'space').astype(jnp.float32)  65.2 us
    ppermute x8, starting transfers between devices, from_behind(): lax.ppermute(value, axis, [(source, source + steps) for source in range(i...  21.1 us
    unnamed x102, local copies, waits for them, and re-layouts  12.1 us
    dot_general x2, matrix products, on_device(): lax.dot_general(flat_grad, w_down[block], contract_cols, preferred_elemen...  11.8 us
    dot_general x2, matrix products, on_device(): lax.dot_general(d_preact, w_up[block], contract_cols, preferred_element_t...  10.1 us
    dot_general x2, matrix products, on_device(): lax.dot_general(hidden, flat_grad, contract_rows, preferred_element_type=...  9.67 us
    dot_general x2, matrix products, on_device(): lax.dot_general(activation, d_preact, contract_rows, preferred_element_ty...  8.18 us
  transfers between devices with their start and end apart: 12, of which 4 were waited for; matrix products, arithmetic and copies ran while one was open for 9% of the time, Pallas kernels for 0%

commit v1 on v0

--- a/solution.py
+++ b/solution.py
@@ -143,7 +143,7 @@
     local_down = jnp.stack(parts_down)
     local_depth = jnp.stack(parts_depth)
     whole = (
-        lax.psum(local_up.astype(jnp.bfloat16), "space").astype(jnp.float32),
+        jnp.sum(lax.all_gather(local_up.astype(jnp.bfloat16), "space"), axis=0).astype(jnp.float32),
         lax.psum(local_down.astype(jnp.bfloat16), "space").astype(jnp.float32),
         lax.psum(local_depth.astype(jnp.bfloat16), "space").astype(jnp.float32),
     )

time: 314 us -> 351 us (1.12)
  waiting for transfers between devices: 111 us -> 132 us
  other arithmetic: 31 us -> 46.3 us
    all_gather x0 -> x1, waiting for transfers between devices: none -> 33.8 us  [on_device(): lax.all_gather(local_up.astype(jnp.bfloat16), 'space')]
    psum x1, waiting for transfers between devices: 99.6 us -> 86.7 us  [on_device(): lax.psum(local_down.astype(jnp.bfloat16), 'space').astype(jnp.float32)]
    reduce_sum x0 -> x1, other arithmetic: none -> 12.6 us  [on_device(): jnp.sum(lax.all_gather(local_up.astype(jnp.bfloat16), 'space'), axis=0)]
  transfers between devices with their start and end apart: 12 -> 13, of which waited for: 4 -> 5; matrix products, arithmetic and copies ran while one was open for 9% -> 12% of each run, Pallas kernels for 0% -> 0%
where the time goes in v1:
time: 351 us; the launch traced here: 350 us
  waiting for transfers between devices  132 us (38%)
  blocking collectives  66.4 us (19%)
  other arithmetic  46.3 us (13%)
  matrix products  42 us (12%)
  local copies, waits for them, and re-layouts  24.7 us (7%)
  starting transfers between devices  21.3 us (6%)
  between operations  17.8 us (5%)
    psum x1, waiting for transfers between devices, on_device(): lax.psum(local_down.astype(jnp.bfloat16), 'space').astype(jnp.float32)  86.7 us
    psum x1, blocking collectives, on_device(): lax.psum(local_depth.astype(jnp.bfloat16), 'space').astype(jnp.float32)  66.4 us
    all_gather x1, waiting for transfers between devices, on_device(): lax.all_gather(local_up.astype(jnp.bfloat16), 'space')  33.8 us
    ppermute x8, starting transfers between devices, from_behind(): lax.ppermute(value, axis, [(source, source + steps) for source in range(i...  21.1 us
    reduce_sum x1, other arithmetic, on_device(): jnp.sum(lax.all_gather(local_up.astype(jnp.bfloat16), 'space'), axis=0)  12.6 us
    unnamed x102, local copies, waits for them, and re-layouts  12.1 us
    dot_general x2, matrix products, on_device(): lax.dot_general(flat_grad, w_down[block], contract_cols, preferred_elemen...  11.8 us
    dot_general x2, matrix products, on_device(): lax.dot_general(d_preact, w_up[block], contract_cols, preferred_element_t...  10.1 us
  transfers between devices with their start and end apart: 13, of which 5 were waited for; matrix products, arithmetic and copies ran while one was open for 12% of the time, Pallas kernels for 0%

profile of v1, /device:TPU:1, one launch (start us, length us, event | category | flops | bytes accessed | tf_op | source)
XLA Modules:
  0.0 350.2 jit_solution(6651649523426975879)
XLA Ops:
  8.8 3.4 multiply_convert_fusion.6
  13.1 4.6 %collective-permute-start = (bf16[1,2,64,256]{3,2,1,0:T(8,128)(2,1)S(1)}, bf16[1,2,64,256]{3,2,1,0:T(8,128)(2,1)S(1)}, u32[]{:S(2)}, u32[]{:S(2)}) collective-permute-start(bf16[1,2,64,256]{3,2,1,0:T(8,128)(2,1)S(1)} %get-tuple-element.95), channel_id=1, source_target_pairs={{0,1},{1,2},{2,3},{3,4},{4,5},{5,6},{6,7},{7,8},{8,9},{9,10},{10,1... | collective-permute-start | bytes 196616 | tf_op jit(solution)/shard_map/ppermute | solution.py:17
  17.7 1.9 collective-permute-start.1
  19.6 1.6 convert_element_type.174
  22.1 1.2 collective-permute-done.1
  23.5 0.6 gather_fusion.1
  24.3 1.4 copy-done.22
  25.6 1.4 pad_maximum_fusion.15
  27.1 1.2 fusion.63
  28.4 0.6 copy-done.11
  29.0 0.6 copy-done.13
  29.7 0.7 copy-done.15
  30.4 0.7 copy-done.17
  31.6 1.3 fusion.81
  33.1 3.0 convolution_add_fusion
  36.1 1.7 fusion.97
  38.5 2.4 collective-permute-start.2
  41.0 2.1 collective-permute-start.3
  43.4 3.2 collective-permute-done.3
  46.6 1.0 maximum_bitcast_fusion.1
  47.6 1.7 gather_fusion.3
  49.5 1.4 copy-done.21
  50.9 1.7 pad_maximum_fusion.11
  54.4 2.2 fusion.22
  56.6 1.3 fusion.76
  58.5 5.9 %fusion.8 = bf16[2048,1024]{1,0:T(8,128)(2,1)S(1)} fusion(f32[2048,1024]{1,0:T(8,128)S(1)} %fusion.76, bf16[2048,256]{1,0:T(8,128)(2,1)S(1)} %bitcast.382, bf16[2,1024,256]{2,1,0:T(8,128)(2,1)S(1)} %copy-done.39), kind=kOutput, calls=%fused_computation.20 | convolution fusion | flops 1113587712 | bytes 14155776 | tf_op jit(solution)/shard_map/dot_general | solution.py:124
  64.5 4.3 %fusion.38 = (bf16[256]{0:T(256)(128)(2,1)S(1)}, bf16[256]{0:T(256)(128)(2,1)S(1)}, bf16[256]{0:T(256)(128)(2,1)S(1)}, bf16[256]{0:T(256)(128)(2,1)S(1)}, bf16[2...) fusion(f32[4,8,8,8,256]{4,3,2,1,0:T(8,128)S(1)} %copy.124, ...), kind=kOutput, calls=%fused_computation.80 | convolution fusion | flops 1083701504 | bytes 20459008 | tf_op jit(solution)/shard_map/dot_general | solution.py:131
  68.8 0.9 copy-done.7
  70.4 1.9 collective-permute-start.4
  72.3 2.8 collective-permute-start.5
  75.1 6.1 %fusion.71 = bf16[1,1024,256]{2,1,0:T(8,128)(2,1)} fusion(bf16[2048,256]{1,0:T(8,128)(2,1)S(1)} %bitcast.383, f32[2048,1024]{1,0:T(8,128)} %copy-done.3), kind=kOutput, calls=%fused_computation.168 | convolution fusion | flops 1092878336 | bytes 9961472 | tf_op jit(solution)/shard_map/dot_general | solution.py:121
  81.2 1.6 convert_element_type.190
  82.9 1.0 maximum_bitcast_fusion.2
  83.9 1.7 gather_fusion.5
  85.8 1.4 copy-done.23
  87.2 1.7 pad_maximum_fusion.7
  88.9 2.2 fusion.31
  91.2 3.6 %fusion.74 = bf16[1,1024,256]{2,1,0:T(8,128)(2,1)S(1)} fusion(bf16[2048,256]{1,0:T(8,128)(2,1)S(1)} %fusion.31, f32[2048,1024]{1,0:T(8,128)S(1)} %bitcast.361), kind=kOutput, calls=%fused_computation.171 | convolution fusion | flops 1092878336 | bytes 9961472 | tf_op jit(solution)/shard_map/dot_general | solution.py:121
  94.9 5.9 %fusion.13 = bf16[2048,1024]{1,0:T(8,128)(2,1)S(1)} fusion(f32[2048,1024]{1,0:T(8,128)S(1)} %bitcast.361, bf16[2048,256]{1,0:T(8,128)(2,1)S(1)} %fusion.31, bf16[2,1024,256]{2,1,0:T(8,128)(2,1)S(1)} %copy-done.40), kind=kOutput, calls=%fused_computation.25 | convolution fusion | flops 1113587712 | bytes 14155776 | tf_op jit(solution)/shard_map/dot_general | solution.py:124
  101.0 5.9 %fusion.52 = (bf16[256]{0:T(256)(128)(2,1)S(1)}, bf16[256]{0:T(256)(128)(2,1)S(1)}, bf16[256]{0:T(256)(128)(2,1)S(1)}, bf16[256]{0:T(256)(128)(2,1)S(1)}, bf16[2...) fusion(f32[4,8,8,8,256]{4,3,2,1,0:T(8,128)S(1)} %copy-done.12, ...), kind=kOutput, calls=%fused_computation.94 | convolution fusion | flops 1090517248 | bytes 20459008 | tf_op jit(solution)/shard_map/dot_general | solution.py:131
  107.1 0.7 reshape.469
  108.0 1.1 pad_maximum_fusion.17
  109.2 3.6 %fusion.73 = bf16[1,1,256,1024]{3,2,1,0:T(8,128)(2,1)S(1)} fusion(bf16[2048,256]{1,0:T(8,128)(2,1)S(1)} %copy-done.26, bf16[2048,1024]{1,0:T(8,128)(2,1)} %copy-done.31), kind=kOutput, calls=%fused_computation.170 | convolution fusion | flops 1074003968 | bytes 5767168 | tf_op jit(solution)/shard_map/dot_general | solution.py:128
  112.9 1.3 fusion.72
  114.2 1.1 pad_maximum_fusion.16
  115.3 1.5 convert_element_type.198
  116.8 1.0 slice_bitcast_fusion.9
  117.8 1.0 fusion.99
  119.5 3.4 collective-permute-start.6
  122.9 1.9 collective-permute-start.7
  124.8 6.7 %reduce-scatter.10.cloned.1.call-done = bf16[64,14]{1,0:T(8,128)(2,1)} async-done(((bf16[256,14]{1,0:T(8,128)(2,1)}), bf16[64,14]{1,0:T(8,128)(2,1)}) %reduce-scatter.10.cloned.1.call-update) | async-done | bytes 1808
  131.6 0.8 reshape.470
  132.5 66.4 %psum.17 = bf16[2,7,64]{2,1,0:T(8,128)(2,1)S(1)} all-reduce(bf16[2,7,64]{2,1,0:T(8,128)(2,1)S(1)} %copy.135), channel_id=1, replica_groups=mesh['rep'=4,'space'=32] {'space'}, use_global_device_ids=true, to_apply=%region_18.19 | all-reduce | flops 896 | bytes 3584 | tf_op jit(solution)/shard_map/psum | solution.py:148
  198.9 0.6 copy.133
  199.6 1.1 maximum_bitcast_fusion.3
  200.7 1.7 gather_fusion.7
  202.4 33.8 %all-gather.2.cloned.1.call-done = bf16[32,2,256,1024]{3,2,1,0:T(8,128)(2,1)} async-done(((bf16[1,2,256,1024]{3,2,1,0:T(8,128)(2,1)}), bf16[32,2,256,1024]{3,2,1,0:T(8,128)(2,1)}) %all-gather.2.cloned.1.call-update) | async-done | bytes 33554448 | tf_op jit(solution)/shard_map/all_gather | solution.py:146
  236.1 12.6 %reduce_sum.138 = bf16[2,256,1024]{2,1,0:T(8,128)(2,1)} reduce(bf16[32,2,256,1024]{3,2,1,0:T(8,128)(2,1)} %all-gather.2.cloned.1.call-done, bf16[]{:T(256)} %constant.12.clone.1), dimensions={0}, to_apply=%region_0.1 | reduce | flops 16252928 | bytes 34603008 | tf_op jit(solution)/shard_map/reduce_sum | solution.py:146
  248.9 1.4 pad_maximum_fusion.3
  250.5 1.1 fusion.45
  251.6 1.2 multiply_convert_fusion.3
  252.8 86.7 %all-reduce.6.cloned.1.call-done = bf16[2,256,256]{2,1,0:T(8,128)(2,1)} async-done(((bf16[2,256,256]{2,1,0:T(8,128)(2,1)}), bf16[2,256,256]{2,1,0:T(8,128)(2,1)}) %all-reduce.6.cloned.1.call-update) | async-done | bytes 262160 | tf_op jit(solution)/shard_map/psum | solution.py:147
  339.5 1.8 convert_multiply_fusion.17
  341.3 1.8 convert_multiply_fusion.18
  (177 shorter events, 8.4 us)
Async XLA Ops:
  8.0 14.0 %copy-start = (f32[1000,256]{1,0:T(8,128)S(1)}, f32[1000,256]{1,0:T(8,128)}, u32[]{:S(2)}) copy-start(f32[1000,256]{1,0:T(8,128)} %param.15) | copy-start | bytes 3072004
  8.0 123.5 %reduce-scatter.10.cloned.1.call-start = ((), (), s32[]{:S(2)}) async-start(), calls=%async_computation.7 | async-start | bytes 81920
  8.8 3.5 copy-start.41
  12.2 14.9 %copy-start.4 = (bf16[4,512,256]{2,1,0:T(8,128)(2,1)}, bf16[4,512,256]{2,1,0:T(8,128)(2,1)S(1)}, u32[]{:S(2)}) copy-start(bf16[4,512,256]{2,1,0:T(8,128)(2,1)S(1)} %get-tuple-element.112) | copy-start | bytes 3145732
  12.5 9.4 %copy-start.37 = (s32[4,4]{1,0:T(4,128)S(1)}, s32[4,4]{1,0:T(4,128)}, u32[]{:S(2)}) copy-start(s32[4,4]{1,0:T(4,128)} %param.19) | copy-start | bytes 196
  12.5 9.5 %copy-start.36 = (f32[2,7,256]{2,0,1:T(2,128)S(1)}, f32[2,7,256]{2,0,1:T(2,128)}, u32[]{:S(2)}) copy-start(f32[2,7,256]{2,0,1:T(2,128)} %param.14) | copy-start | bytes 43012
  13.1 9.0 %collective-permute-start = (bf16[1,2,64,256]{3,2,1,0:T(8,128)(2,1)S(1)}, bf16[1,2,64,256]{3,2,1,0:T(8,128)(2,1)S(1)}, u32[]{:S(2)}, u32[]{:S(2)}) collective-permute-start(bf16[1,2,64,256]{3,2,1,0:T(8,128)(2,1)S(1)} %get-tuple-element.95), channel_id=1, source_target_pairs={{0,1},{1,2},{2,3},{3,4},{4,5},{5,6},{6,7},{7,8},{8,9},{9,10},{10,1... | collective-permute-start | bytes 196616 | tf_op jit(solution)/shard_map/ppermute | solution.py:17
  17.7 5.6 %collective-permute-start.1 = (bf16[1,2,64,256]{3,2,1,0:T(8,128)(2,1)S(1)}, bf16[1,2,64,256]{3,2,1,0:T(8,128)(2,1)S(1)}, u32[]{:S(2)}, u32[]{:S(2)}) collective-permute-start(bf16[1,2,64,256]{3,2,1,0:T(8,128)(2,1)S(1)} %get-tuple-element.96), channel_id=1, source_target_pairs={{1,0},{2,1},{3,2},{4,3},{5,4},{6,5},{7,6},{8,7},{9,8},{10,9},{11,1... | collective-permute-start | bytes 196616 | tf_op jit(solution)/shard_map/ppermute | solution.py:17
  24.0 1.6 copy-start.22
  27.1 1.4 copy-start.9
  27.1 2.0 copy-start.11
  27.1 2.6 copy-start.13
  27.1 3.3 copy-start.15
  27.1 3.9 %copy-start.17 = (f32[4,8,8,8,256]{4,3,2,1,0:T(8,128)}, f32[4,8,8,8,256]{4,3,2,1,0:T(8,128)S(1)}, u32[]{:S(2)}) copy-start(f32[4,8,8,8,256]{4,3,2,1,0:T(8,128)S(1)} %get-tuple-element.55) | copy-start | bytes 6291460
  27.1 4.5 %copy-start.19 = (f32[4,8,8,8,256]{4,3,2,1,0:T(8,128)}, f32[4,8,8,8,256]{4,3,2,1,0:T(8,128)S(1)}, u32[]{:S(2)}) copy-start(f32[4,8,8,8,256]{4,3,2,1,0:T(8,128)S(1)} %get-tuple-element.56) | copy-start | bytes 6291460
  27.1 4.5 %copy-start.32 = (bf16[2,256,1024]{2,1,0:T(8,128)(2,1)S(1)}, bf16[2,256,1024]{2,1,0:T(8,128)(2,1)}, u32[]{:S(2)}) copy-start(bf16[2,256,1024]{2,1,0:T(8,128)(2,1)} %param.12) | copy-start | bytes 3145732
  31.6 1.3 copy-start.5
  31.6 1.5 copy-start.38
  32.8 3.3 copy-start.2
  38.5 4.8 %collective-permute-start.2 = (bf16[1,2,64,256]{3,2,1,0:T(8,128)(2,1)S(1)}, bf16[1,2,64,256]{3,2,1,0:T(8,128)(2,1)S(1)}, u32[]{:S(2)}, u32[]{:S(2)}) collective-permute-start(bf16[1,2,64,256]{3,2,1,0:T(8,128)(2,1)S(1)} %get-tuple-element.93), channel_id=1, source_target_pairs={{0,1},{1,2},{2,3},{3,4},{4,5},{5,6},{6,7},{7,8},{8,9},{9,10},{10,1... | collective-permute-start | bytes 196616 | tf_op jit(solution)/shard_map/ppermute | solution.py:17
  41.0 5.6 %collective-permute-start.3 = (bf16[1,2,64,256]{3,2,1,0:T(8,128)(2,1)S(1)}, bf16[1,2,64,256]{3,2,1,0:T(8,128)(2,1)S(1)}, u32[]{:S(2)}, u32[]{:S(2)}) collective-permute-start(bf16[1,2,64,256]{3,2,1,0:T(8,128)(2,1)S(1)} %get-tuple-element.94), channel_id=1, source_target_pairs={{1,0},{2,1},{3,2},{4,3},{5,4},{6,5},{7,6},{8,7},{9,8},{10,9},{11,1... | collective-permute-start | bytes 196616 | tf_op jit(solution)/shard_map/ppermute | solution.py:17
  49.3 1.6 copy-start.21
  54.4 2.2 copy-start.33
  56.6 1.3 copy-start.25
  56.6 1.6 copy-start.27
  56.6 1.9 copy-start.39
  57.9 6.5 %copy-start.3 = (f32[2048,1024]{1,0:T(8,128)}, f32[2048,1024]{1,0:T(8,128)S(1)}, u32[]{:S(2)}) copy-start(f32[2048,1024]{1,0:T(8,128)S(1)} %fusion.76) | copy-start | bytes 25165828
  64.5 4.3 %copy-start.31 = (bf16[2048,1024]{1,0:T(8,128)(2,1)}, bf16[2048,1024]{1,0:T(8,128)(2,1)S(1)}, u32[]{:S(2)}) copy-start(bf16[2048,1024]{1,0:T(8,128)(2,1)S(1)} %fusion.8) | copy-start | bytes 12582916
  68.7 1.0 copy-start.7
  68.8 6.4 %copy-start.28 = (bf16[4,512,256]{2,1,0:T(8,128)(2,1)S(1)}, bf16[4,512,256]{2,1,0:T(8,128)(2,1)}, u32[]{:S(2)}) copy-start(bf16[4,512,256]{2,1,0:T(8,128)(2,1)} %get-tuple-element.111) | copy-start | bytes 3145732
  70.4 12.5 %collective-permute-start.4 = (bf16[1,2,64,256]{3,2,1,0:T(8,128)(2,1)S(1)}, bf16[1,2,64,256]{3,2,1,0:T(8,128)(2,1)S(1)}, u32[]{:S(2)}, u32[]{:S(2)}) collective-permute-start(bf16[1,2,64,256]{3,2,1,0:T(8,128)(2,1)S(1)} %get-tuple-element.91), channel_id=1, source_target_pairs={{0,1},{1,2},{2,3},{3,4},{4,5},{5,6},{6,7},{7,8},{8,9},{9,10},{10,1... | collective-permute-start | bytes 196616 | tf_op jit(solution)/shard_map/ppermute | solution.py:17
  72.3 8.9 %copy-start.8 = (bf16[2048,256]{1,0:T(8,128)(2,1)S(1)}, bf16[2048,256]{1,0:T(8,128)(2,1)}, u32[]{:S(2)}) copy-start(bf16[2048,256]{1,0:T(8,128)(2,1)} %copy-done.7) | copy-start | bytes 3145732
  72.3 10.6 %collective-permute-start.5 = (bf16[1,2,64,256]{3,2,1,0:T(8,128)(2,1)S(1)}, bf16[1,2,64,256]{3,2,1,0:T(8,128)(2,1)S(1)}, u32[]{:S(2)}, u32[]{:S(2)}) collective-permute-start(bf16[1,2,64,256]{3,2,1,0:T(8,128)(2,1)S(1)} %get-tuple-element.92), channel_id=1, source_target_pairs={{1,0},{2,1},{3,2},{4,3},{5,4},{6,5},{7,6},{8,7},{9,8},{10,9},{11,1... | collective-permute-start | bytes 196616 | tf_op jit(solution)/shard_map/ppermute | solution.py:17
  85.6 1.6 copy-start.23
  87.2 4.0 %slice-start = ((s8[8388608]{0:T(1024)(128)(4,1)}), s8[4194304]{0:T(1024)(128)(4,1)S(1)}, s32[]{:S(2)}) async-start(s8[8388608]{0:T(1024)(128)(4,1)} %bitcast.360), calls=%async_computation.8 | async-start | bytes 8388608
  88.9 2.3 slice-start.1
  91.2 3.6 %copy-start.29 = (bf16[2048,256]{1,0:T(8,128)(2,1)}, bf16[2048,256]{1,0:T(8,128)(2,1)S(1)}, u32[]{:S(2)}) copy-start(bf16[2048,256]{1,0:T(8,128)(2,1)S(1)} %fusion.31) | copy-start | bytes 3145732
  91.2 3.6 %copy-start.40 = (bf16[2,1024,256]{2,1,0:T(8,128)(2,1)S(1)}, bf16[2,1024,256]{2,1,0:T(8,128)(2,1)}, u32[]{:S(2)}) copy-start(bf16[2,1024,256]{2,1,0:T(8,128)(2,1)} %param.13) | copy-start | bytes 3145732
  94.8 6.0 %copy-start.6 = (bf16[4,512,256]{2,1,0:T(8,128)(2,1)S(1)}, bf16[4,512,256]{2,1,0:T(8,128)(2,1)}, u32[]{:S(2)}) copy-start(bf16[4,512,256]{2,1,0:T(8,128)(2,1)} %copy-done.4) | copy-start | bytes 3145732
  94.9 6.0 %copy-start.10 = (f32[4,8,8,8,256]{4,3,2,1,0:T(8,128)S(1)}, f32[4,8,8,8,256]{4,3,2,1,0:T(8,128)}, u32[]{:S(2)}) copy-start(f32[4,8,8,8,256]{4,3,2,1,0:T(8,128)} %copy-done.9) | copy-start | bytes 6291460
  94.9 6.0 %copy-start.12 = (f32[4,8,8,8,256]{4,3,2,1,0:T(8,128)S(1)}, f32[4,8,8,8,256]{4,3,2,1,0:T(8,128)}, u32[]{:S(2)}) copy-start(f32[4,8,8,8,256]{4,3,2,1,0:T(8,128)} %copy-done.11) | copy-start | bytes 6291460
  94.9 6.0 %copy-start.14 = (f32[4,8,8,8,256]{4,3,2,1,0:T(8,128)S(1)}, f32[4,8,8,8,256]{4,3,2,1,0:T(8,128)}, u32[]{:S(2)}) copy-start(f32[4,8,8,8,256]{4,3,2,1,0:T(8,128)} %copy-done.13) | copy-start | bytes 6291460
  94.9 6.0 %copy-start.16 = (f32[4,8,8,8,256]{4,3,2,1,0:T(8,128)S(1)}, f32[4,8,8,8,256]{4,3,2,1,0:T(8,128)}, u32[]{:S(2)}) copy-start(f32[4,8,8,8,256]{4,3,2,1,0:T(8,128)} %copy-done.15) | copy-start | bytes 6291460
  94.9 6.0 %copy-start.18 = (f32[4,8,8,8,256]{4,3,2,1,0:T(8,128)S(1)}, f32[4,8,8,8,256]{4,3,2,1,0:T(8,128)}, u32[]{:S(2)}) copy-start(f32[4,8,8,8,256]{4,3,2,1,0:T(8,128)} %copy-done.17) | copy-start | bytes 6291460
  94.9 6.0 %copy-start.20 = (f32[4,8,8,8,256]{4,3,2,1,0:T(8,128)S(1)}, f32[4,8,8,8,256]{4,3,2,1,0:T(8,128)}, u32[]{:S(2)}) copy-start(f32[4,8,8,8,256]{4,3,2,1,0:T(8,128)} %copy-done.19) | copy-start | bytes 6291460
  94.9 6.0 %copy-start.34 = (bf16[2,256,1024]{2,1,0:T(8,128)(2,1)S(1)}, bf16[2,256,1024]{2,1,0:T(8,128)(2,1)}, u32[]{:S(2)}) copy-start(bf16[2,256,1024]{2,1,0:T(8,128)(2,1)} %param.12) | copy-start | bytes 3145732
  100.9 5.9 %copy-start.42 = (bf16[2048,1024]{1,0:T(8,128)(2,1)}, bf16[2048,1024]{1,0:T(8,128)(2,1)S(1)}, u32[]{:S(2)}) copy-start(bf16[2048,1024]{1,0:T(8,128)(2,1)S(1)} %fusion.13) | copy-start | bytes 12582916
  100.9 7.0 %copy-start.35 = (bf16[1,1024,256]{2,1,0:T(8,128)(2,1)S(1)}, bf16[1,1024,256]{2,1,0:T(8,128)(2,1)}, u32[]{:S(2)}) copy-start(bf16[1,1024,256]{2,1,0:T(8,128)(2,1)} %fusion.71) | copy-start | bytes 1572868
  106.8 2.4 copy-start.26
  107.9 91.6 %reduce-scatter.8.cloned.1.call-start = ((), (), s32[]{:S(2)}) async-start(), calls=%async_computation.5 | async-start | bytes 1310720 | tf_op jit(solution)/shard_map/reduce_scatter | solution.py:154
  109.1 3.7 %copy-start.44 = (bf16[2048,256]{1,0:T(8,128)(2,1)S(1)}, bf16[2048,256]{1,0:T(8,128)(2,1)}, u32[]{:S(2)}) copy-start(bf16[2048,256]{1,0:T(8,128)(2,1)} %get-tuple-element.32) | copy-start | bytes 3145732
  109.1 127.0 %all-gather.2.cloned.1.call-start = ((), (), s32[]{:S(2)}) async-start(), calls=%async_computation.3 | async-start | bytes 34603008 | tf_op jit(solution)/shard_map/all_gather | solution.py:146
  109.2 3.7 %copy-start.43 = (bf16[2048,1024]{1,0:T(8,128)(2,1)S(1)}, bf16[2048,1024]{1,0:T(8,128)(2,1)}, u32[]{:S(2)}) copy-start(bf16[2048,1024]{1,0:T(8,128)(2,1)} %copy-done.42) | copy-start | bytes 12582916
  115.3 224.2 %all-reduce.6.cloned.1.call-start = ((), (), s32[]{:S(2)}) async-start(), calls=%async_computation.6 | async-start | bytes 524288 | tf_op jit(solution)/shard_map/psum | solution.py:147
  119.5 80.1 %collective-permute-start.6 = (bf16[1,2,64,256]{3,2,1,0:T(8,128)(2,1)S(1)}, bf16[1,2,64,256]{3,2,1,0:T(8,128)(2,1)S(1)}, u32[]{:S(2)}, u32[]{:S(2)}) collective-permute-start(bf16[1,2,64,256]{3,2,1,0:T(8,128)(2,1)S(1)} %get-tuple-element.89), channel_id=1, source_target_pairs={{0,1},{1,2},{2,3},{3,4},{4,5},{5,6},{6,7},{7,8},{8,9},{9,10},{10,1... | collective-permute-start | bytes 196616 | tf_op jit(solution)/shard_map/ppermute | solution.py:17
  122.9 76.7 %collective-permute-start.7 = (bf16[1,2,64,256]{3,2,1,0:T(8,128)(2,1)S(1)}, bf16[1,2,64,256]{3,2,1,0:T(8,128)(2,1)S(1)}, u32[]{:S(2)}, u32[]{:S(2)}) collective-permute-start(bf16[1,2,64,256]{3,2,1,0:T(8,128)(2,1)S(1)} %get-tuple-element.90), channel_id=1, source_target_pairs={{1,0},{2,1},{3,2},{4,3},{5,4},{6,5},{7,6},{8,7},{9,8},{10,9},{11,1... | collective-permute-start | bytes 196616 | tf_op jit(solution)/shard_map/ppermute | solution.py:17
  199.5 141.8 %reduce-scatter.6.cloned.1.call-start = ((), (), s32[]{:S(2)}) async-start(), calls=%async_computation.4 | async-start | bytes 1310720 | tf_op jit(solution)/shard_map/reduce_scatter | solution.py:151
  248.9 1.5 copy-start.24
  248.9 1.5 copy-start.30
  251.6 91.5 %copy-start.1 = (f32[1000,256]{1,0:T(8,128)S(1)}, f32[1000,256]{1,0:T(8,128)}, u32[]{:S(2)}) copy-start(f32[1000,256]{1,0:T(8,128)} %param.15) | copy-start | bytes 3072004
Sparse Core Ops, SparseCore 0:
  108.0 23.4 reduce-scatter.9
  134.1 24.1 reduce-scatter.7
  248.8 20.5 reduce-scatter.5
Sparse Core Ops, SparseCore 1:
  115.4 120.7 all-gather.1
  239.6 99.9 all-reduce.5
